TPU v7x, 128 devices: a whole 4x4x4 slice. The times are simulated.
128 devices in a mesh: lon: 16 (over x_hi, z, core), lat: 8 (over x_lo, y).
Axes of the slice: x: 4 (x_hi: 2, x_lo: 2; x = x_hi * 2 + x_lo), y: 4, z: 4, core: 2. Of those that a mesh axis runs over, the one named last changes fastest.
Arguments:
- state: bfloat16 [16, 8, 64, 512, 128], P('lon', 'lat'), may hold values from -6 to 6
- conv_w: bfloat16 [3, 8, 16, 16], replicated, may hold values from -0.875 to 0.875
- readout: float32 [128, 8], replicated, may hold values from -0.5 to 0.5
- kernel: float32 [256, 64, 8], replicated, may hold values from -0.25 to 0.25
- cross_col: int32 [16, 8, 8, 256], P('lon', 'lat'), may hold values from 0 to 511
- seg_count: int32 [16, 8, 256], P('lon', 'lat'), may hold values from 1 to 8
- seg_len: float32 [16, 8, 8, 256], P('lon', 'lat'), may hold values from 0.25 to 1
- observed: float32 [16, 8, 256, 256], P('lon', 'lat'), may hold values from -8 to 8
- obs_err: float32 [16, 8, 256, 256], P('lon', 'lat'), may hold values from 0.5 to 2
Outputs:
- grad_state: bfloat16 [16, 8, 64, 512, 128], P('lon', 'lat')
- bending: float32 [16, 8, 256, 256], P('lon', 'lat')
- grad_conv: float32 [3, 8, 16, 16], replicated
Inputs may be any that keep to these rules, and one draw needn't show every extreme that they name: `cross_col`: a column of the crossed tile.
All inputs are finite; a program needn't handle non-finite values.
Results may differ from a plain program's by a relative error of at most 0.0037.
The roundings to bfloat16 on the way count: a program that leaves them out, or rounds other values in their place, can miss the bound.
Values sent between devices are 32-bit elements; how exact they have to be, the bound alone decides.
A program may use at most 192 MiB of HBM per device.

v0:
```python
import jax
import jax.numpy as jnp
from jax import lax
from jax.sharding import PartitionSpec as P


def from_behind(value, axis, steps):
    count = lax.axis_size(axis)
    pairs = [(source, (source + steps) % count) for source in range(count)]
    return lax.ppermute(value, axis, pairs)


def block_weights(conv_w):
    taps, groups, width, _ = conv_w.shape
    eye = jnp.eye(groups, dtype=jnp.float32)
    full = conv_w.astype(jnp.float32)[:, :, :, None, :] * eye[None, :, None, :, None]
    return full.reshape(taps, groups * width, groups * width).astype(jnp.bfloat16)


def on_device(state, conv_w, readout, kernel, cross_col, seg_count, seg_len, observed, obs_err):
    column = state[0, 0]
    levels = column.shape[0]
    ncols = column.shape[1]
    taps = conv_w.shape[0]
    groups = conv_w.shape[1]
    width = conv_w.shape[2]
    wide = block_weights(conv_w)
    padded = jnp.pad(column, ((1, 1), (0, 0), (0, 0)))
    act = jnp.zeros(column.shape, jnp.float32)
    for tap in range(taps):
        act = act + jnp.einsum(
            "lci,ij->lcj", padded[tap : tap + levels], wide[tap], preferred_element_type=jnp.float32
        )
    feat = jax.nn.silu(act)
    profile = jnp.einsum("lcj,jn->cln", feat, readout, precision=lax.Precision.HIGHEST).reshape(
        ncols, -1
    )
    span = cross_col.shape[2]
    rays = cross_col.shape[3]
    lon_n = lax.axis_size("lon")
    here = lax.axis_index("lon")
    every = lax.all_gather(seg_count, "lon", axis=0, tiled=True)[:, 0, :]
    offsets = jnp.arange(span, dtype=jnp.int32)
    owners = (here - offsets) % lon_n
    counts = jnp.take(every, owners, axis=0)
    weight = seg_len[0, 0] * (offsets[:, None] < counts).astype(jnp.float32)
    places = cross_col[0, 0].reshape(-1)
    sampled = jnp.take(profile, places, axis=0).reshape(span, rays, -1) * weight[:, :, None]
    kflat = kernel.reshape(kernel.shape[0], -1)
    carried = sampled[span - 1]
    for step in range(span - 2, -1, -1):
        carried = from_behind(carried, "lon", -1) + sampled[step]
    bending = jnp.einsum("rq,kq->rk", carried, kflat, precision=lax.Precision.HIGHEST)
    adjoint = (bending - observed[0, 0]) / (obs_err[0, 0] * obs_err[0, 0])
    current = jnp.dot(adjoint, kflat, precision=lax.Precision.HIGHEST)
    held = [current]
    for step in range(1, span):
        current = from_behind(current, "lon", 1)
        held.append(current)
    back = jnp.stack(held)
    back = back * weight[:, :, None]
    dprofile = (
        jnp.zeros((ncols, back.shape[2]), jnp.float32)
        .at[places]
        .add(back.reshape(-1, back.shape[2]))
    )
    dfeat = jnp.einsum(
        "cln,jn->lcj", dprofile.reshape(ncols, levels, -1), readout, precision=lax.Precision.HIGHEST
    )
    sig = jax.nn.sigmoid(act)
    dact = (dfeat * sig * (1.0 + act * (1.0 - sig))).astype(jnp.bfloat16)
    dpad = jnp.pad(dact, ((1, 1), (0, 0), (0, 0)))
    grad_x = jnp.zeros(column.shape, jnp.float32)
    grads = []
    for tap in range(taps):
        grad_x = grad_x + jnp.einsum(
            "lcj,ij->lci",
            dpad[2 - tap : 2 - tap + levels],
            wide[tap],
            preferred_element_type=jnp.float32,
        )
        grads.append(
            jnp.einsum(
                "lci,lcj->ij", padded[tap : tap + levels], dact, preferred_element_type=jnp.float32
            )
        )
    grad_w = jnp.stack(grads).reshape(taps, groups, width, groups, width)
    eye = jnp.eye(groups, dtype=jnp.float32)
    grouped = jnp.einsum("tgahb,gh->tgab", grad_w, eye)
    grad_conv = lax.psum(grouped, ("lon", "lat"))
    return (grad_x.astype(jnp.bfloat16)[None, None], bending[None, None], grad_conv)


def solution(mesh):
    in_specs = (
        P("lon", "lat", None, None, None),
        P(),
        P(),
        P(),
        P("lon", "lat", None, None),
        P("lon", "lat", None),
        P("lon", "lat", None, None),
        P("lon", "lat", None, None),
        P("lon", "lat", None, None),
    )
    out_specs = (P("lon", "lat", None, None, None), P("lon", "lat", None, None), P())
    return jax.shard_map(
        on_device, mesh=mesh, in_specs=in_specs, out_specs=out_specs, check_vma=False
    )
```

profile of v0, /device:TPU:1, one launch (start us, length us, event | category | flops | bytes accessed | tf_op | source)
XLA Modules:
  0.0 433.3 jit_solution(11439077147525505158)
XLA Ops:
  2.5 11.4 %fusion.8 = f32[64,512,128]{2,1,0:T(8,128)} fusion(bf16[1,1,64,512,128]{4,3,2,1,0:T(8,128)(2,1)} %param.9, bf16[3,128,128]{2,1,0:T(8,128)(2,1)S(1)} %multiply_convert_fusion), kind=kOutput, calls=%fused_computation.15 | convolution fusion | flops 1056964608 | bytes 25198592 | tf_op jit(solution)/shard_map/lci,ij->lcj/dot_general | solution.py:31
  14.0 11.4 %fusion.12 = f32[128,64,512]{0,2,1:T(8,128)} fusion(bf16[1,1,64,512,128]{4,3,2,1,0:T(8,128)(2,1)} %param.9, bf16[3,128,128]{2,1,0:T(8,128)(2,1)S(1)} %multiply_convert_fusion), kind=kOutput, calls=%fused_computation.19 | convolution fusion | flops 1073741824 | bytes 25198592 | tf_op jit(solution)/shard_map/lci,ij->lcj/dot_general | solution.py:31
  25.5 21.0 %fusion.2 = f32[64,512,128]{2,1,0:T(8,128)} fusion(f32[64,512,128]{2,1,0:T(8,128)} %fusion.8, f32[128,64,512]{0,2,1:T(8,128)} %fusion.12, bf16[1,1,64,512,128]{4,3,2,1,0:T(8,128)(2,1)} %param.9, bf16[3,128,128]{2,1,0:T(8,128)(2,1)S(1)} %multiply_convert_fusion), kind=kOutput, calls=%fused_computation.7 | convolution fusion | flops 1065353216 | bytes 58753024 | tf_op jit(solution)/shard_map/lci,ij->lcj/dot_general | solution.py:31
  46.5 21.1 %fusion.20 = f32[512,512]{0,1:T(8,128)S(1)} fusion(f32[64,512,128]{2,1,0:T(8,128)} %fusion.2, f32[128,8]{0,1:T(8,128)S(1)} %copy-done.9), kind=kOutput, calls=%fused_computation.30 | convolution fusion | flops 419430400 | bytes 17829888 | tf_op jit(solution)/shard_map/lcj,jn->cln/dot_general | solution.py:35
  68.0 26.7 %all_gather.3 = s32[16,1,256]{2,1,0:T(1,128)S(1)} all-gather(s32[1,1,256]{2,1,0:T(1,128)S(1)} %copy-done.8), channel_id=1, replica_groups=mesh['lon'=16,'lat'=8] {'lon'}, dimensions={0}, use_global_device_ids=true | all-gather | bytes 17408 | tf_op jit(solution)/shard_map/all_gather | solution.py:42
  94.7 8.9 %gather_fusion = f32[2048,512]{1,0:T(8,128)} fusion(f32[512,512]{1,0:T(8,128)S(1)} %copy.40, s32[2048]{0:T(1024)S(1)} %broadcast_clamp_fusion), kind=kCustom, calls=%fused_computation | custom fusion | bytes 8396800 | tf_op jit(solution)/shard_map/jit(_take)/gather | solution.py:48
  104.3 2.7 select_multiply_fusion
  107.2 8.4 %collective-permute-done = f32[256,512]{1,0:T(8,128)S(1)} collective-permute-done((f32[256,512]{1,0:T(8,128)S(1)}, f32[256,512]{1,0:T(8,128)S(1)}, u32[]{:S(2)}, u32[]{:S(2)}) %collective-permute-start) | collective-permute-done | bytes 524320 | tf_op jit(solution)/shard_map/ppermute | solution.py:10
  115.8 8.6 %collective-permute-done.1 = f32[256,512]{1,0:T(8,128)S(1)} collective-permute-done((f32[256,512]{1,0:T(8,128)S(1)}, f32[256,512]{1,0:T(8,128)S(1)}, u32[]{:S(2)}, u32[]{:S(2)}) %collective-permute-start.1) | collective-permute-done | bytes 524320 | tf_op jit(solution)/shard_map/ppermute | solution.py:10
  126.5 6.7 %collective-permute-done.2 = f32[256,512]{1,0:T(8,128)S(1)} collective-permute-done((f32[256,512]{1,0:T(8,128)S(1)}, f32[256,512]{1,0:T(8,128)S(1)}, u32[]{:S(2)}, u32[]{:S(2)}) %collective-permute-start.2) | collective-permute-done | bytes 524320 | tf_op jit(solution)/shard_map/ppermute | solution.py:10
  133.3 5.6 %collective-permute-start.3 = (f32[256,512]{1,0:T(8,128)S(1)}, f32[256,512]{1,0:T(8,128)S(1)}, u32[]{:S(2)}, u32[]{:S(2)}) collective-permute-start(f32[256,512]{1,0:T(8,128)S(1)} %fusion.39), channel_id=1, source_target_pairs={{0,120},{8,0},{16,8},{24,16},{32,24},{40,32},{48,40},{56,48},{64,5... | collective-permute-start | bytes 1572872 | tf_op jit(solution)/shard_map/ppermute | solution.py:10
  138.9 3.1 collective-permute-done.3
  142.0 9.2 %collective-permute-start.4 = (f32[256,512]{1,0:T(8,128)S(1)}, f32[256,512]{1,0:T(8,128)S(1)}, u32[]{:S(2)}, u32[]{:S(2)}) collective-permute-start(f32[256,512]{1,0:T(8,128)S(1)} %fusion.38), channel_id=1, source_target_pairs={{0,120},{8,0},{16,8},{24,16},{32,24},{40,32},{48,40},{56,48},{64,5... | collective-permute-start | bytes 1572872 | tf_op jit(solution)/shard_map/ppermute | solution.py:10
  152.9 10.8 %collective-permute-start.5 = (f32[256,512]{1,0:T(8,128)S(1)}, f32[256,512]{1,0:T(8,128)S(1)}, u32[]{:S(2)}, u32[]{:S(2)}) collective-permute-start(f32[256,512]{1,0:T(8,128)S(1)} %fusion.37), channel_id=1, source_target_pairs={{0,120},{8,0},{16,8},{24,16},{32,24},{40,32},{48,40},{56,48},{64,5... | collective-permute-start | bytes 1572872 | tf_op jit(solution)/shard_map/ppermute | solution.py:10
  165.2 11.0 %collective-permute-start.6 = (f32[256,512]{1,0:T(8,128)S(1)}, f32[256,512]{1,0:T(8,128)S(1)}, u32[]{:S(2)}, u32[]{:S(2)}) collective-permute-start(f32[256,512]{1,0:T(8,128)S(1)} %fusion.36), channel_id=1, source_target_pairs={{0,120},{8,0},{16,8},{24,16},{32,24},{40,32},{48,40},{56,48},{64,5... | collective-permute-start | bytes 1572872 | tf_op jit(solution)/shard_map/ppermute | solution.py:10
  179.9 12.1 %collective-permute-done.7 = f32[256,512]{1,0:T(8,128)S(1)} collective-permute-done((f32[256,512]{1,0:T(8,128)S(1)}, f32[256,512]{1,0:T(8,128)S(1)}, u32[]{:S(2)}, u32[]{:S(2)}) %collective-permute-start.7) | collective-permute-done | bytes 524320 | tf_op jit(solution)/shard_map/ppermute | solution.py:10
  191.9 12.4 %collective-permute-done.8 = f32[256,512]{1,0:T(8,128)S(1)} collective-permute-done((f32[256,512]{1,0:T(8,128)S(1)}, f32[256,512]{1,0:T(8,128)S(1)}, u32[]{:S(2)}, u32[]{:S(2)}) %collective-permute-start.8) | collective-permute-done | bytes 524320 | tf_op jit(solution)/shard_map/ppermute | solution.py:10
  204.3 12.2 %collective-permute-done.9 = f32[256,512]{1,0:T(8,128)S(1)} collective-permute-done((f32[256,512]{1,0:T(8,128)S(1)}, f32[256,512]{1,0:T(8,128)S(1)}, u32[]{:S(2)}, u32[]{:S(2)}) %collective-permute-start.9) | collective-permute-done | bytes 524320 | tf_op jit(solution)/shard_map/ppermute | solution.py:10
  216.5 12.2 %collective-permute-done.10 = f32[256,512]{1,0:T(8,128)S(1)} collective-permute-done((f32[256,512]{1,0:T(8,128)S(1)}, f32[256,512]{1,0:T(8,128)S(1)}, u32[]{:S(2)}, u32[]{:S(2)}) %collective-permute-start.10) | collective-permute-done | bytes 524320 | tf_op jit(solution)/shard_map/ppermute | solution.py:10
  228.8 12.2 %collective-permute-done.11 = f32[256,512]{1,0:T(8,128)S(1)} collective-permute-done((f32[256,512]{1,0:T(8,128)S(1)}, f32[256,512]{1,0:T(8,128)S(1)}, u32[]{:S(2)}, u32[]{:S(2)}) %collective-permute-start.11) | collective-permute-done | bytes 524320 | tf_op jit(solution)/shard_map/ppermute | solution.py:10
  243.5 9.7 %collective-permute-done.12 = f32[256,512]{1,0:T(8,128)S(1)} collective-permute-done((f32[256,512]{1,0:T(8,128)S(1)}, f32[256,512]{1,0:T(8,128)S(1)}, u32[]{:S(2)}, u32[]{:S(2)}) %collective-permute-start.12) | collective-permute-done | bytes 524320 | tf_op jit(solution)/shard_map/ppermute | solution.py:10
  255.7 9.7 %collective-permute-done.13 = f32[256,512]{1,0:T(8,128)S(1)} collective-permute-done((f32[256,512]{1,0:T(8,128)S(1)}, f32[256,512]{1,0:T(8,128)S(1)}, u32[]{:S(2)}, u32[]{:S(2)}) %collective-permute-start.13) | collective-permute-done | bytes 524320 | tf_op jit(solution)/shard_map/ppermute | solution.py:10
  266.3 4.5 %bitcast_multiply_fusion.1 = f32[2048,512]{1,0:T(8,128)} fusion(f32[8,256,512]{2,1,0:T(8,128)} %bitcast_dynamic-update-slice_fusion, f32[2048]{0:T(1024)S(1)} %broadcast_select_fusion), kind=kLoop, calls=%fused_computation.25 | loop fusion | flops 1048576 | bytes 8396800 | tf_op jit(solution)/shard_map/mul | solution.py:61
  270.7 13.9 %scatter_custom_fusion = f32[512,512]{1,0:T(8,128)S(1)} fusion(s32[2048]{0:T(1024)S(1)} %bitcast.183, f32[2048,512]{1,0:T(8,128)} %bitcast_multiply_fusion.1, f32[]{:T(128)} %constant.51.clone.1), kind=kCustom, calls=%fused_computation.62 | custom fusion | flops 1048576 | bytes 1049088 | tf_op jit(solution)/shard_map/scatter-add | solution.py:65
  285.0 31.4 %fusion.1 = bf16[64,512,128]{2,1,0:T(8,128)(2,1)S(1)} fusion(f32[64,512,128]{2,1,0:T(8,128)} %fusion.2, f32[512,512]{0,1:T(8,128)S(1)} %copy.41, f32[128,8]{0,1:T(8,128)S(1)} %copy-done.9), kind=kOutput, calls=%fused_computation.5 | convolution fusion | flops 440401920 | bytes 26218496 | tf_op jit(solution)/shard_map/cln,jn->lcj/dot_general | solution.py:67
  316.4 7.4 %fusion.48 = f32[64,512,128]{2,1,0:T(8,128)} fusion(bf16[64,512,128]{2,1,0:T(8,128)(2,1)S(1)} %fusion.1, bf16[3,128,128]{2,1,0:T(8,128)(2,1)S(1)} %multiply_convert_fusion), kind=kOutput, calls=%fused_computation.73 | convolution fusion | flops 1056964608 | bytes 25198592 | tf_op jit(solution)/shard_map/lcj,ij->lci/dot_general | solution.py:76
  323.9 8.3 %fusion.49 = f32[64,512,128]{2,1,0:T(8,128)} fusion(bf16[64,512,128]{2,1,0:T(8,128)(2,1)S(1)} %fusion.1, bf16[3,128,128]{2,1,0:T(8,128)(2,1)S(1)} %multiply_convert_fusion), kind=kOutput, calls=%fused_computation.74 | convolution fusion | flops 1073741824 | bytes 25198592 | tf_op jit(solution)/shard_map/lcj,ij->lci/dot_general | solution.py:76
  332.2 2.4 fusion.23
  334.6 2.4 fusion.26
  337.0 2.4 fusion.29
  340.6 74.6 %psum.7 = f32[3,8,16,16]{3,2,1,0:T(8,128)} all-reduce(f32[3,8,16,16]{3,2,1,0:T(8,128)S(1)} %bitcast.179), channel_id=1, replica_groups=mesh['lon'=16,'lat'=8] {'lon','lat'}, use_global_device_ids=true, to_apply=%region_1.2 | all-reduce | flops 6144 | bytes 49152 | tf_op jit(solution)/shard_map/psum | solution.py:90
  415.3 17.8 %fusion.17 = bf16[1,1,64,512,128]{4,3,2,1,0:T(8,128)(2,1)} fusion(bf16[64,512,128]{2,1,0:T(8,128)(2,1)} %copy-done.2, f32[64,512,128]{2,1,0:T(8,128)} %fusion.48, f32[64,512,128]{2,1,0:T(8,128)} %fusion.49, bf16[3,128,128]{2,1,0:T(8,128)(2,1)S(1)} %multiply_convert_fusion), kind=kOutput, calls=%fused_computation.24 | convolution fusion | flops 1069547520 | bytes 50364416 | tf_op jit(solution)/shard_map/lcj,ij->lci/dot_general | solution.py:76
  (82 shorter events, 19.9 us)
Async XLA Ops:
  0.6 177.1 %copy-start = (f32[256,64,8]{0,2,1:T(8,128)S(1)}, f32[256,64,8]{0,2,1:T(8,128)}, u32[]{:S(2)}) copy-start(f32[256,64,8]{0,2,1:T(8,128)} %param.12) | copy-start | bytes 1572868
  14.0 11.5 %copy-start.6 = (s32[1,1,8,256]{3,2,1,0:T(8,128)S(1)}, s32[1,1,8,256]{3,2,1,0:T(8,128)}, u32[]{:S(2)}) copy-start(s32[1,1,8,256]{3,2,1,0:T(8,128)} %param.13) | copy-start | bytes 24580
  25.5 21.0 %copy-start.9 = (f32[128,8]{0,1:T(8,128)S(1)}, f32[128,8]{0,1:T(8,128)}, u32[]{:S(2)}) copy-start(f32[128,8]{0,1:T(8,128)} %param.11) | copy-start | bytes 12292
  46.5 21.5 %copy-start.8 = (s32[1,1,256]{2,1,0:T(1,128)S(1)}, s32[1,1,256]{2,1,0:T(1,128)}, u32[]{:S(2)}) copy-start(s32[1,1,256]{2,1,0:T(1,128)} %param.14) | copy-start | bytes 3076
  94.7 9.5 %copy-start.7 = (f32[1,1,8,256]{3,2,1,0:T(8,128)S(1)}, f32[1,1,8,256]{3,2,1,0:T(8,128)}, u32[]{:S(2)}) copy-start(f32[1,1,8,256]{3,2,1,0:T(8,128)} %param.15) | copy-start | bytes 24580
  104.3 74.1 %copy-start.4 = (f32[1,1,256,256]{3,2,1,0:T(8,128)S(1)}, f32[1,1,256,256]{3,2,1,0:T(8,128)}, u32[]{:S(2)}) copy-start(f32[1,1,256,256]{3,2,1,0:T(8,128)} %param.16) | copy-start | bytes 786436
  104.3 74.1 %copy-start.5 = (f32[1,1,256,256]{3,2,1,0:T(8,128)S(1)}, f32[1,1,256,256]{3,2,1,0:T(8,128)}, u32[]{:S(2)}) copy-start(f32[1,1,256,256]{3,2,1,0:T(8,128)} %param.17) | copy-start | bytes 786436
  107.0 8.7 %collective-permute-start = (f32[256,512]{1,0:T(8,128)S(1)}, f32[256,512]{1,0:T(8,128)S(1)}, u32[]{:S(2)}, u32[]{:S(2)}) collective-permute-start(f32[256,512]{1,0:T(8,128)S(1)} %slice_bitcast_fusion.7), channel_id=1, source_target_pairs={{0,120},{8,0},{16,8},{24,16},{32,24},{40,32},{48,40},{56,48},{64,5... | collective-permute-start | bytes 1572872 | tf_op jit(solution)/shard_map/ppermute | solution.py:10
  115.8 8.7 %collective-permute-start.1 = (f32[256,512]{1,0:T(8,128)S(1)}, f32[256,512]{1,0:T(8,128)S(1)}, u32[]{:S(2)}, u32[]{:S(2)}) collective-permute-start(f32[256,512]{1,0:T(8,128)S(1)} %fusion.41), channel_id=1, source_target_pairs={{0,120},{8,0},{16,8},{24,16},{32,24},{40,32},{48,40},{56,48},{64,5... | collective-permute-start | bytes 1572872 | tf_op jit(solution)/shard_map/ppermute | solution.py:10
  124.5 8.7 %collective-permute-start.2 = (f32[256,512]{1,0:T(8,128)S(1)}, f32[256,512]{1,0:T(8,128)S(1)}, u32[]{:S(2)}, u32[]{:S(2)}) collective-permute-start(f32[256,512]{1,0:T(8,128)S(1)} %fusion.40), channel_id=1, source_target_pairs={{0,120},{8,0},{16,8},{24,16},{32,24},{40,32},{48,40},{56,48},{64,5... | collective-permute-start | bytes 1572872 | tf_op jit(solution)/shard_map/ppermute | solution.py:10
  133.3 8.7 %collective-permute-start.3 = (f32[256,512]{1,0:T(8,128)S(1)}, f32[256,512]{1,0:T(8,128)S(1)}, u32[]{:S(2)}, u32[]{:S(2)}) collective-permute-start(f32[256,512]{1,0:T(8,128)S(1)} %fusion.39), channel_id=1, source_target_pairs={{0,120},{8,0},{16,8},{24,16},{32,24},{40,32},{48,40},{56,48},{64,5... | collective-permute-start | bytes 1572872 | tf_op jit(solution)/shard_map/ppermute | solution.py:10
  142.0 10.7 %collective-permute-start.4 = (f32[256,512]{1,0:T(8,128)S(1)}, f32[256,512]{1,0:T(8,128)S(1)}, u32[]{:S(2)}, u32[]{:S(2)}) collective-permute-start(f32[256,512]{1,0:T(8,128)S(1)} %fusion.38), channel_id=1, source_target_pairs={{0,120},{8,0},{16,8},{24,16},{32,24},{40,32},{48,40},{56,48},{64,5... | collective-permute-start | bytes 1572872 | tf_op jit(solution)/shard_map/ppermute | solution.py:10
  152.9 12.3 %collective-permute-start.5 = (f32[256,512]{1,0:T(8,128)S(1)}, f32[256,512]{1,0:T(8,128)S(1)}, u32[]{:S(2)}, u32[]{:S(2)}) collective-permute-start(f32[256,512]{1,0:T(8,128)S(1)} %fusion.37), channel_id=1, source_target_pairs={{0,120},{8,0},{16,8},{24,16},{32,24},{40,32},{48,40},{56,48},{64,5... | collective-permute-start | bytes 1572872 | tf_op jit(solution)/shard_map/ppermute | solution.py:10
  165.2 12.5 %collective-permute-start.6 = (f32[256,512]{1,0:T(8,128)S(1)}, f32[256,512]{1,0:T(8,128)S(1)}, u32[]{:S(2)}, u32[]{:S(2)}) collective-permute-start(f32[256,512]{1,0:T(8,128)S(1)} %fusion.36), channel_id=1, source_target_pairs={{0,120},{8,0},{16,8},{24,16},{32,24},{40,32},{48,40},{56,48},{64,5... | collective-permute-start | bytes 1572872 | tf_op jit(solution)/shard_map/ppermute | solution.py:10
  178.4 92.4 %copy-start.3 = (f32[256,256]{1,0:T(8,128)}, f32[256,256]{1,0:T(8,128)S(1)}, u32[]{:S(2)}) copy-start(f32[256,256]{1,0:T(8,128)S(1)} %fusion.34) | copy-start | bytes 786436
  179.9 12.1 %collective-permute-start.7 = (f32[256,512]{1,0:T(8,128)S(1)}, f32[256,512]{1,0:T(8,128)S(1)}, u32[]{:S(2)}, u32[]{:S(2)}) collective-permute-start(f32[256,512]{1,0:T(8,128)S(1)} %get-tuple-element.6), channel_id=1, source_target_pairs={{0,8},{8,16},{16,24},{24,32},{32,40},{40,48},{48,56},{56,64},{64,7... | collective-permute-start | bytes 1572872 | tf_op jit(solution)/shard_map/ppermute | solution.py:10
  191.9 12.4 %collective-permute-start.8 = (f32[256,512]{1,0:T(8,128)S(1)}, f32[256,512]{1,0:T(8,128)S(1)}, u32[]{:S(2)}, u32[]{:S(2)}) collective-permute-start(f32[256,512]{1,0:T(8,128)S(1)} %collective-permute-done.7), channel_id=1, source_target_pairs={{0,8},{8,16},{16,24},{24,32},{32,40},{40,48},{48,56},{56,64},{64,7... | collective-permute-start | bytes 1572872 | tf_op jit(solution)/shard_map/ppermute | solution.py:10
  204.3 12.2 %collective-permute-start.9 = (f32[256,512]{1,0:T(8,128)S(1)}, f32[256,512]{1,0:T(8,128)S(1)}, u32[]{:S(2)}, u32[]{:S(2)}) collective-permute-start(f32[256,512]{1,0:T(8,128)S(1)} %collective-permute-done.8), channel_id=1, source_target_pairs={{0,8},{8,16},{16,24},{24,32},{32,40},{40,48},{48,56},{56,64},{64,7... | collective-permute-start | bytes 1572872 | tf_op jit(solution)/shard_map/ppermute | solution.py:10
  216.5 12.2 %collective-permute-start.10 = (f32[256,512]{1,0:T(8,128)S(1)}, f32[256,512]{1,0:T(8,128)S(1)}, u32[]{:S(2)}, u32[]{:S(2)}) collective-permute-start(f32[256,512]{1,0:T(8,128)S(1)} %collective-permute-done.9), channel_id=1, source_target_pairs={{0,8},{8,16},{16,24},{24,32},{32,40},{40,48},{48,56},{56,64},{64,7... | collective-permute-start | bytes 1572872 | tf_op jit(solution)/shard_map/ppermute | solution.py:10
  228.8 12.2 %collective-permute-start.11 = (f32[256,512]{1,0:T(8,128)S(1)}, f32[256,512]{1,0:T(8,128)S(1)}, u32[]{:S(2)}, u32[]{:S(2)}) collective-permute-start(f32[256,512]{1,0:T(8,128)S(1)} %collective-permute-done.10), channel_id=1, source_target_pairs={{0,8},{8,16},{16,24},{24,32},{32,40},{40,48},{48,56},{56,64},{64,7... | collective-permute-start | bytes 1572872 | tf_op jit(solution)/shard_map/ppermute | solution.py:10
  241.0 12.2 %collective-permute-start.12 = (f32[256,512]{1,0:T(8,128)S(1)}, f32[256,512]{1,0:T(8,128)S(1)}, u32[]{:S(2)}, u32[]{:S(2)}) collective-permute-start(f32[256,512]{1,0:T(8,128)S(1)} %collective-permute-done.11), channel_id=1, source_target_pairs={{0,8},{8,16},{16,24},{24,32},{32,40},{40,48},{48,56},{56,64},{64,7... | collective-permute-start | bytes 1572872 | tf_op jit(solution)/shard_map/ppermute | solution.py:10
  253.2 12.2 %collective-permute-start.13 = (f32[256,512]{1,0:T(8,128)S(1)}, f32[256,512]{1,0:T(8,128)S(1)}, u32[]{:S(2)}, u32[]{:S(2)}) collective-permute-start(f32[256,512]{1,0:T(8,128)S(1)} %collective-permute-done.12), channel_id=1, source_target_pairs={{0,8},{8,16},{16,24},{24,32},{32,40},{40,48},{48,56},{56,64},{64,7... | collective-permute-start | bytes 1572872 | tf_op jit(solution)/shard_map/ppermute | solution.py:10
  316.4 20.5 %copy-start.2 = (bf16[64,512,128]{2,1,0:T(8,128)(2,1)}, bf16[64,512,128]{2,1,0:T(8,128)(2,1)S(1)}, u32[]{:S(2)}) copy-start(bf16[64,512,128]{2,1,0:T(8,128)(2,1)S(1)} %fusion.1) | copy-start | bytes 25165828
  316.4 15.7 %slice-start = ((s8[8388608]{0:T(1024)(128)(4,1)}), s8[4194304]{0:T(1024)(128)(4,1)S(1)}, s32[]{:S(2)}) async-start(s8[8388608]{0:T(1024)(128)(4,1)} %bitcast.175), calls=%async_computation | async-start | bytes 8388608
  323.9 8.3 %slice-start.1 = ((s8[8388608]{0:T(1024)(128)(4,1)}), s8[4194304]{0:T(1024)(128)(4,1)S(1)}, s32[]{:S(2)}) async-start(s8[8388608]{0:T(1024)(128)(4,1)} %bitcast.175), calls=%async_computation.1 | async-start | bytes 8388608
  415.3 17.8 %copy-start.1 = (f32[256,64,8]{0,2,1:T(8,128)S(1)}, f32[256,64,8]{0,2,1:T(8,128)}, u32[]{:S(2)}) copy-start(f32[256,64,8]{0,2,1:T(8,128)} %param.12) | copy-start | bytes 1572868
where the time goes:
time: 440 us; the launch traced here: 433 us
  matrix products  139 us (32%)
  waiting for transfers between devices  112 us (25%)
  blocking collectives  101 us (23%)
  starting transfers between devices  38.8 us (9%)
  other arithmetic  21.7 us (5%)
  local copies, waits for them, and re-layouts  18.8 us (4%)
    ppermute x14, waiting for transfers between devices, from_behind(): return lax.ppermute(value, axis, pairs)  112 us
    psum x1, blocking collectives, on_device(): grad_conv = lax.psum(grouped, ('lon', 'lat'))  74.6 us
    dot_general x3, matrix products, on_device(): jnp.einsum('lci,ij->lcj', padded[tap:tap + levels], wide[tap], preferred_...  43.8 us
    ppermute x14, starting transfers between devices, from_behind(): return lax.ppermute(value, axis, pairs)  38.8 us
    dot_general x3, matrix products, on_device(): jnp.einsum('lcj,ij->lci', dpad[2 - tap:2 - tap + levels], wide[tap], pref...  33.5 us
    dot_general x1, matrix products, on_device(): jnp.einsum('cln,jn->lcj', dprofile.reshape(ncols, levels, -1), readout, p...  31.4 us
    all_gather x1, blocking collectives, on_device(): every = lax.all_gather(seg_count, 'lon', axis=0, tiled=True)[:, 0, :]  26.7 us
    dot_general x1, matrix products, on_device(): jnp.einsum('lcj,jn->cln', feat, readout, precision=lax.Precision.HIGHEST)  21.1 us
  transfers between devices with their start and end apart: 14, of which 14 were waited for; matrix products, arithmetic and copies ran while one was open for 1% of the time, Pallas kernels for 0%

commit v1 on v0

--- a/solution.py
+++ b/solution.py
@@ -87,7 +87,7 @@
     grad_w = jnp.stack(grads).reshape(taps, groups, width, groups, width)
     eye = jnp.eye(groups, dtype=jnp.float32)
     grouped = jnp.einsum("tgahb,gh->tgab", grad_w, eye)
-    grad_conv = lax.psum(grouped, ("lon", "lat"))
+    grad_conv = lax.psum(lax.psum(grouped, "lon"), "lat")
     return (grad_x.astype(jnp.bfloat16)[None, None], bending[None, None], grad_conv)
 
 

time: 440 us -> 477 us (1.084)
  the two profiles are of different devices: /device:TPU:1 before, /device:TPU:0 now
where the time goes in v1:
time: 477 us; the launch traced here: 471 us
  matrix products  139 us (29%)
  blocking collectives  128 us (27%)
  waiting for transfers between devices  128 us (27%)
  starting transfers between devices  33.8 us (7%)
  other arithmetic  21.7 us (5%)
  local copies, waits for them, and re-layouts  18.8 us (4%)
    ppermute x14, waiting for transfers between devices, from_behind(): return lax.ppermute(value, axis, pairs)  128 us
    psum x2, blocking collectives, on_device(): grad_conv = lax.psum(lax.psum(grouped, 'lon'), 'lat')  103 us
    dot_general x3, matrix products, on_device(): jnp.einsum('lci,ij->lcj', padded[tap:tap + levels], wide[tap], preferred_...  43.8 us
    ppermute x14, starting transfers between devices, from_behind(): return lax.ppermute(value, axis, pairs)  33.8 us
    dot_general x3, matrix products, on_device(): jnp.einsum('lcj,ij->lci', dpad[2 - tap:2 - tap + levels], wide[tap], pref...  33.5 us
    dot_general x1, matrix products, on_device(): jnp.einsum('cln,jn->lcj', dprofile.reshape(ncols, levels, -1), readout, p...  31.4 us
    all_gather x1, blocking collectives, on_device(): every = lax.all_gather(seg_count, 'lon', axis=0, tiled=True)[:, 0, :]  25.5 us
    dot_general x1, matrix products, on_device(): jnp.einsum('lcj,jn->cln', feat, readout, precision=lax.Precision.HIGHEST)  21.1 us
  transfers between devices with their start and end apart: 14, of which 14 were waited for; matrix products, arithmetic and copies ran while one was open for 1% of the time, Pallas kernels for 0%

profile of v1, /device:TPU:0, one launch (start us, length us, event | category | flops | bytes accessed | tf_op | source)
XLA Modules:
  0.0 470.5 jit_solution(17908573242112060605)
XLA Ops:
  2.5 11.4 %fusion.8 = f32[64,512,128]{2,1,0:T(8,128)} fusion(bf16[1,1,64,512,128]{4,3,2,1,0:T(8,128)(2,1)} %param.9, bf16[3,128,128]{2,1,0:T(8,128)(2,1)S(1)} %multiply_convert_fusion), kind=kOutput, calls=%fused_computation.15 | convolution fusion | flops 1056964608 | bytes 25198592 | tf_op jit(solution)/shard_map/lci,ij->lcj/dot_general | solution.py:31
  14.0 11.4 %fusion.12 = f32[128,64,512]{0,2,1:T(8,128)} fusion(bf16[1,1,64,512,128]{4,3,2,1,0:T(8,128)(2,1)} %param.9, bf16[3,128,128]{2,1,0:T(8,128)(2,1)S(1)} %multiply_convert_fusion), kind=kOutput, calls=%fused_computation.19 | convolution fusion | flops 1073741824 | bytes 25198592 | tf_op jit(solution)/shard_map/lci,ij->lcj/dot_general | solution.py:31
  25.5 21.0 %fusion.2 = f32[64,512,128]{2,1,0:T(8,128)} fusion(f32[64,512,128]{2,1,0:T(8,128)} %fusion.8, f32[128,64,512]{0,2,1:T(8,128)} %fusion.12, bf16[1,1,64,512,128]{4,3,2,1,0:T(8,128)(2,1)} %param.9, bf16[3,128,128]{2,1,0:T(8,128)(2,1)S(1)} %multiply_convert_fusion), kind=kOutput, calls=%fused_computation.7 | convolution fusion | flops 1065353216 | bytes 58753024 | tf_op jit(solution)/shard_map/lci,ij->lcj/dot_general | solution.py:31
  46.5 21.1 %fusion.20 = f32[512,512]{0,1:T(8,128)S(1)} fusion(f32[64,512,128]{2,1,0:T(8,128)} %fusion.2, f32[128,8]{0,1:T(8,128)S(1)} %copy-done.9), kind=kOutput, calls=%fused_computation.30 | convolution fusion | flops 419430400 | bytes 17829888 | tf_op jit(solution)/shard_map/lcj,jn->cln/dot_general | solution.py:35
  67.9 25.5 %all_gather.3 = s32[16,1,256]{2,1,0:T(1,128)S(1)} all-gather(s32[1,1,256]{2,1,0:T(1,128)S(1)} %copy-done.8), channel_id=1, replica_groups=mesh['lon'=16,'lat'=8] {'lon'}, dimensions={0}, use_global_device_ids=true | all-gather | bytes 17408 | tf_op jit(solution)/shard_map/all_gather | solution.py:42
  93.5 8.9 %gather_fusion = f32[2048,512]{1,0:T(8,128)} fusion(f32[512,512]{1,0:T(8,128)S(1)} %copy.40, s32[2048]{0:T(1024)S(1)} %broadcast_clamp_fusion), kind=kCustom, calls=%fused_computation | custom fusion | bytes 8396800 | tf_op jit(solution)/shard_map/jit(_take)/gather | solution.py:48
  105.8 6.7 %collective-permute-done = f32[256,512]{1,0:T(8,128)S(1)} collective-permute-done((f32[256,512]{1,0:T(8,128)S(1)}, f32[256,512]{1,0:T(8,128)S(1)}, u32[]{:S(2)}, u32[]{:S(2)}) %collective-permute-start) | collective-permute-done | bytes 524320 | tf_op jit(solution)/shard_map/ppermute | solution.py:10
  112.6 5.6 %collective-permute-start.1 = (f32[256,512]{1,0:T(8,128)S(1)}, f32[256,512]{1,0:T(8,128)S(1)}, u32[]{:S(2)}, u32[]{:S(2)}) collective-permute-start(f32[256,512]{1,0:T(8,128)S(1)} %fusion.41), channel_id=1, source_target_pairs={{0,120},{8,0},{16,8},{24,16},{32,24},{40,32},{48,40},{56,48},{64,5... | collective-permute-start | bytes 1572872 | tf_op jit(solution)/shard_map/ppermute | solution.py:10
  118.2 6.7 %collective-permute-done.1 = f32[256,512]{1,0:T(8,128)S(1)} collective-permute-done((f32[256,512]{1,0:T(8,128)S(1)}, f32[256,512]{1,0:T(8,128)S(1)}, u32[]{:S(2)}, u32[]{:S(2)}) %collective-permute-start.1) | collective-permute-done | bytes 524320 | tf_op jit(solution)/shard_map/ppermute | solution.py:10
  124.9 5.6 %collective-permute-start.2 = (f32[256,512]{1,0:T(8,128)S(1)}, f32[256,512]{1,0:T(8,128)S(1)}, u32[]{:S(2)}, u32[]{:S(2)}) collective-permute-start(f32[256,512]{1,0:T(8,128)S(1)} %fusion.40), channel_id=1, source_target_pairs={{0,120},{8,0},{16,8},{24,16},{32,24},{40,32},{48,40},{56,48},{64,5... | collective-permute-start | bytes 1572872 | tf_op jit(solution)/shard_map/ppermute | solution.py:10
  130.5 6.7 %collective-permute-done.2 = f32[256,512]{1,0:T(8,128)S(1)} collective-permute-done((f32[256,512]{1,0:T(8,128)S(1)}, f32[256,512]{1,0:T(8,128)S(1)}, u32[]{:S(2)}, u32[]{:S(2)}) %collective-permute-start.2) | collective-permute-done | bytes 524320 | tf_op jit(solution)/shard_map/ppermute | solution.py:10
  137.3 5.6 %collective-permute-start.3 = (f32[256,512]{1,0:T(8,128)S(1)}, f32[256,512]{1,0:T(8,128)S(1)}, u32[]{:S(2)}, u32[]{:S(2)}) collective-permute-start(f32[256,512]{1,0:T(8,128)S(1)} %fusion.39), channel_id=1, source_target_pairs={{0,120},{8,0},{16,8},{24,16},{32,24},{40,32},{48,40},{56,48},{64,5... | collective-permute-start | bytes 1572872 | tf_op jit(solution)/shard_map/ppermute | solution.py:10
  142.9 6.7 %collective-permute-done.3 = f32[256,512]{1,0:T(8,128)S(1)} collective-permute-done((f32[256,512]{1,0:T(8,128)S(1)}, f32[256,512]{1,0:T(8,128)S(1)}, u32[]{:S(2)}, u32[]{:S(2)}) %collective-permute-start.3) | collective-permute-done | bytes 524320 | tf_op jit(solution)/shard_map/ppermute | solution.py:10
  149.7 5.6 %collective-permute-start.4 = (f32[256,512]{1,0:T(8,128)S(1)}, f32[256,512]{1,0:T(8,128)S(1)}, u32[]{:S(2)}, u32[]{:S(2)}) collective-permute-start(f32[256,512]{1,0:T(8,128)S(1)} %fusion.38), channel_id=1, source_target_pairs={{0,120},{8,0},{16,8},{24,16},{32,24},{40,32},{48,40},{56,48},{64,5... | collective-permute-start | bytes 1572872 | tf_op jit(solution)/shard_map/ppermute | solution.py:10
  155.3 6.7 %collective-permute-done.4 = f32[256,512]{1,0:T(8,128)S(1)} collective-permute-done((f32[256,512]{1,0:T(8,128)S(1)}, f32[256,512]{1,0:T(8,128)S(1)}, u32[]{:S(2)}, u32[]{:S(2)}) %collective-permute-start.4) | collective-permute-done | bytes 524320 | tf_op jit(solution)/shard_map/ppermute | solution.py:10
  167.7 6.7 %collective-permute-done.5 = f32[256,512]{1,0:T(8,128)S(1)} collective-permute-done((f32[256,512]{1,0:T(8,128)S(1)}, f32[256,512]{1,0:T(8,128)S(1)}, u32[]{:S(2)}, u32[]{:S(2)}) %collective-permute-start.5) | collective-permute-done | bytes 524320 | tf_op jit(solution)/shard_map/ppermute | solution.py:10
  174.4 5.8 %collective-permute-start.6 = (f32[256,512]{1,0:T(8,128)S(1)}, f32[256,512]{1,0:T(8,128)S(1)}, u32[]{:S(2)}, u32[]{:S(2)}) collective-permute-start(f32[256,512]{1,0:T(8,128)S(1)} %fusion.36), channel_id=1, source_target_pairs={{0,120},{8,0},{16,8},{24,16},{32,24},{40,32},{48,40},{56,48},{64,5... | collective-permute-start | bytes 1572872 | tf_op jit(solution)/shard_map/ppermute | solution.py:10
  180.2 6.7 %collective-permute-done.6 = f32[256,512]{1,0:T(8,128)S(1)} collective-permute-done((f32[256,512]{1,0:T(8,128)S(1)}, f32[256,512]{1,0:T(8,128)S(1)}, u32[]{:S(2)}, u32[]{:S(2)}) %collective-permute-start.6) | collective-permute-done | bytes 524320 | tf_op jit(solution)/shard_map/ppermute | solution.py:10
  189.1 12.4 %collective-permute-done.7 = f32[256,512]{1,0:T(8,128)S(1)} collective-permute-done((f32[256,512]{1,0:T(8,128)S(1)}, f32[256,512]{1,0:T(8,128)S(1)}, u32[]{:S(2)}, u32[]{:S(2)}) %collective-permute-start.7) | collective-permute-done | bytes 524320 | tf_op jit(solution)/shard_map/ppermute | solution.py:10
  201.5 12.2 %collective-permute-done.8 = f32[256,512]{1,0:T(8,128)S(1)} collective-permute-done((f32[256,512]{1,0:T(8,128)S(1)}, f32[256,512]{1,0:T(8,128)S(1)}, u32[]{:S(2)}, u32[]{:S(2)}) %collective-permute-start.8) | collective-permute-done | bytes 524320 | tf_op jit(solution)/shard_map/ppermute | solution.py:10
  213.7 12.2 %collective-permute-done.9 = f32[256,512]{1,0:T(8,128)S(1)} collective-permute-done((f32[256,512]{1,0:T(8,128)S(1)}, f32[256,512]{1,0:T(8,128)S(1)}, u32[]{:S(2)}, u32[]{:S(2)}) %collective-permute-start.9) | collective-permute-done | bytes 524320 | tf_op jit(solution)/shard_map/ppermute | solution.py:10
  225.9 12.2 %collective-permute-done.10 = f32[256,512]{1,0:T(8,128)S(1)} collective-permute-done((f32[256,512]{1,0:T(8,128)S(1)}, f32[256,512]{1,0:T(8,128)S(1)}, u32[]{:S(2)}, u32[]{:S(2)}) %collective-permute-start.10) | collective-permute-done | bytes 524320 | tf_op jit(solution)/shard_map/ppermute | solution.py:10
  238.2 12.2 %collective-permute-done.11 = f32[256,512]{1,0:T(8,128)S(1)} collective-permute-done((f32[256,512]{1,0:T(8,128)S(1)}, f32[256,512]{1,0:T(8,128)S(1)}, u32[]{:S(2)}, u32[]{:S(2)}) %collective-permute-start.11) | collective-permute-done | bytes 524320 | tf_op jit(solution)/shard_map/ppermute | solution.py:10
  252.8 9.7 %collective-permute-done.12 = f32[256,512]{1,0:T(8,128)S(1)} collective-permute-done((f32[256,512]{1,0:T(8,128)S(1)}, f32[256,512]{1,0:T(8,128)S(1)}, u32[]{:S(2)}, u32[]{:S(2)}) %collective-permute-start.12) | collective-permute-done | bytes 524320 | tf_op jit(solution)/shard_map/ppermute | solution.py:10
  265.0 9.7 %collective-permute-done.13 = f32[256,512]{1,0:T(8,128)S(1)} collective-permute-done((f32[256,512]{1,0:T(8,128)S(1)}, f32[256,512]{1,0:T(8,128)S(1)}, u32[]{:S(2)}, u32[]{:S(2)}) %collective-permute-start.13) | collective-permute-done | bytes 524320 | tf_op jit(solution)/shard_map/ppermute | solution.py:10
  280.1 13.9 %scatter_custom_fusion = f32[512,512]{1,0:T(8,128)S(1)} fusion(s32[2048]{0:T(1024)S(1)} %bitcast.183, f32[2048,512]{1,0:T(8,128)} %bitcast_multiply_fusion.1, f32[]{:T(128)} %constant.51.clone.1), kind=kCustom, calls=%fused_computation.62 | custom fusion | flops 1048576 | bytes 1049088 | tf_op jit(solution)/shard_map/scatter-add | solution.py:65
  294.3 31.4 %fusion.1 = bf16[64,512,128]{2,1,0:T(8,128)(2,1)S(1)} fusion(f32[64,512,128]{2,1,0:T(8,128)} %fusion.2, f32[512,512]{0,1:T(8,128)S(1)} %copy.41, f32[128,8]{0,1:T(8,128)S(1)} %copy-done.9), kind=kOutput, calls=%fused_computation.5 | convolution fusion | flops 440401920 | bytes 26218496 | tf_op jit(solution)/shard_map/cln,jn->lcj/dot_general | solution.py:67
  325.8 7.4 %fusion.48 = f32[64,512,128]{2,1,0:T(8,128)} fusion(bf16[64,512,128]{2,1,0:T(8,128)(2,1)S(1)} %fusion.1, bf16[3,128,128]{2,1,0:T(8,128)(2,1)S(1)} %multiply_convert_fusion), kind=kOutput, calls=%fused_computation.73 | convolution fusion | flops 1056964608 | bytes 25198592 | tf_op jit(solution)/shard_map/lcj,ij->lci/dot_general | solution.py:76
  333.2 8.2 %fusion.49 = f32[64,512,128]{2,1,0:T(8,128)} fusion(bf16[64,512,128]{2,1,0:T(8,128)(2,1)S(1)} %fusion.1, bf16[3,128,128]{2,1,0:T(8,128)(2,1)S(1)} %multiply_convert_fusion), kind=kOutput, calls=%fused_computation.74 | convolution fusion | flops 1073741824 | bytes 25198592 | tf_op jit(solution)/shard_map/lcj,ij->lci/dot_general | solution.py:76
  350.0 66.5 %psum.14 = f32[3,8,16,16]{3,2,1,0:T(8,128)S(1)} all-reduce(f32[3,8,16,16]{3,2,1,0:T(8,128)S(1)} %bitcast.179), channel_id=1, replica_groups=mesh['lon'=16,'lat'=8] {'lon'}, use_global_device_ids=true, to_apply=%region_1.2 | all-reduce | flops 6144 | bytes 49152 | tf_op jit(solution)/shard_map/psum | solution.py:90
  416.4 36.1 %psum.15 = f32[3,8,16,16]{3,2,1,0:T(8,128)} all-reduce(f32[3,8,16,16]{3,2,1,0:T(8,128)S(1)} %psum.14), channel_id=1, replica_groups=mesh['lon'=16,'lat'=8] {'lat'}, use_global_device_ids=true, to_apply=%region_2.3 | all-reduce | flops 6144 | bytes 49152 | tf_op jit(solution)/shard_map/psum | solution.py:90
  452.5 17.8 %fusion.17 = bf16[1,1,64,512,128]{4,3,2,1,0:T(8,128)(2,1)} fusion(bf16[64,512,128]{2,1,0:T(8,128)(2,1)} %copy-done.2, f32[64,512,128]{2,1,0:T(8,128)} %fusion.48, f32[64,512,128]{2,1,0:T(8,128)} %fusion.49, bf16[3,128,128]{2,1,0:T(8,128)(2,1)S(1)} %multiply_convert_fusion), kind=kOutput, calls=%fused_computation.24 | convolution fusion | flops 1069547520 | bytes 50364416 | tf_op jit(solution)/shard_map/lcj,ij->lci/dot_general | solution.py:76
  (83 shorter events, 32.9 us)
Async XLA Ops:
  0.6 186.3 %copy-start = (f32[256,64,8]{0,2,1:T(8,128)S(1)}, f32[256,64,8]{0,2,1:T(8,128)}, u32[]{:S(2)}) copy-start(f32[256,64,8]{0,2,1:T(8,128)} %param.12) | copy-start | bytes 1572868
  14.0 11.5 %copy-start.6 = (s32[1,1,8,256]{3,2,1,0:T(8,128)S(1)}, s32[1,1,8,256]{3,2,1,0:T(8,128)}, u32[]{:S(2)}) copy-start(s32[1,1,8,256]{3,2,1,0:T(8,128)} %param.13) | copy-start | bytes 24580
  25.5 21.0 %copy-start.9 = (f32[128,8]{0,1:T(8,128)S(1)}, f32[128,8]{0,1:T(8,128)}, u32[]{:S(2)}) copy-start(f32[128,8]{0,1:T(8,128)} %param.11) | copy-start | bytes 12292
  46.5 21.5 %copy-start.8 = (s32[1,1,256]{2,1,0:T(1,128)S(1)}, s32[1,1,256]{2,1,0:T(1,128)}, u32[]{:S(2)}) copy-start(s32[1,1,256]{2,1,0:T(1,128)} %param.14) | copy-start | bytes 3076
  93.5 9.5 %copy-start.7 = (f32[1,1,8,256]{3,2,1,0:T(8,128)S(1)}, f32[1,1,8,256]{3,2,1,0:T(8,128)}, u32[]{:S(2)}) copy-start(f32[1,1,8,256]{3,2,1,0:T(8,128)} %param.15) | copy-start | bytes 24580
  103.0 84.6 %copy-start.4 = (f32[1,1,256,256]{3,2,1,0:T(8,128)S(1)}, f32[1,1,256,256]{3,2,1,0:T(8,128)}, u32[]{:S(2)}) copy-start(f32[1,1,256,256]{3,2,1,0:T(8,128)} %param.16) | copy-start | bytes 786436
  103.0 84.6 %copy-start.5 = (f32[1,1,256,256]{3,2,1,0:T(8,128)S(1)}, f32[1,1,256,256]{3,2,1,0:T(8,128)}, u32[]{:S(2)}) copy-start(f32[1,1,256,256]{3,2,1,0:T(8,128)} %param.17) | copy-start | bytes 786436
  105.7 6.8 %collective-permute-start = (f32[256,512]{1,0:T(8,128)S(1)}, f32[256,512]{1,0:T(8,128)S(1)}, u32[]{:S(2)}, u32[]{:S(2)}) collective-permute-start(f32[256,512]{1,0:T(8,128)S(1)} %slice_bitcast_fusion.7), channel_id=1, source_target_pairs={{0,120},{8,0},{16,8},{24,16},{32,24},{40,32},{48,40},{56,48},{64,5... | collective-permute-start | bytes 1572872 | tf_op jit(solution)/shard_map/ppermute | solution.py:10
  112.6 12.3 %collective-permute-start.1 = (f32[256,512]{1,0:T(8,128)S(1)}, f32[256,512]{1,0:T(8,128)S(1)}, u32[]{:S(2)}, u32[]{:S(2)}) collective-permute-start(f32[256,512]{1,0:T(8,128)S(1)} %fusion.41), channel_id=1, source_target_pairs={{0,120},{8,0},{16,8},{24,16},{32,24},{40,32},{48,40},{56,48},{64,5... | collective-permute-start | bytes 1572872 | tf_op jit(solution)/shard_map/ppermute | solution.py:10
  124.9 12.3 %collective-permute-start.2 = (f32[256,512]{1,0:T(8,128)S(1)}, f32[256,512]{1,0:T(8,128)S(1)}, u32[]{:S(2)}, u32[]{:S(2)}) collective-permute-start(f32[256,512]{1,0:T(8,128)S(1)} %fusion.40), channel_id=1, source_target_pairs={{0,120},{8,0},{16,8},{24,16},{32,24},{40,32},{48,40},{56,48},{64,5... | collective-permute-start | bytes 1572872 | tf_op jit(solution)/shard_map/ppermute | solution.py:10
  137.3 12.3 %collective-permute-start.3 = (f32[256,512]{1,0:T(8,128)S(1)}, f32[256,512]{1,0:T(8,128)S(1)}, u32[]{:S(2)}, u32[]{:S(2)}) collective-permute-start(f32[256,512]{1,0:T(8,128)S(1)} %fusion.39), channel_id=1, source_target_pairs={{0,120},{8,0},{16,8},{24,16},{32,24},{40,32},{48,40},{56,48},{64,5... | collective-permute-start | bytes 1572872 | tf_op jit(solution)/shard_map/ppermute | solution.py:10
  149.7 12.3 %collective-permute-start.4 = (f32[256,512]{1,0:T(8,128)S(1)}, f32[256,512]{1,0:T(8,128)S(1)}, u32[]{:S(2)}, u32[]{:S(2)}) collective-permute-start(f32[256,512]{1,0:T(8,128)S(1)} %fusion.38), channel_id=1, source_target_pairs={{0,120},{8,0},{16,8},{24,16},{32,24},{40,32},{48,40},{56,48},{64,5... | collective-permute-start | bytes 1572872 | tf_op jit(solution)/shard_map/ppermute | solution.py:10
  162.1 12.3 %collective-permute-start.5 = (f32[256,512]{1,0:T(8,128)S(1)}, f32[256,512]{1,0:T(8,128)S(1)}, u32[]{:S(2)}, u32[]{:S(2)}) collective-permute-start(f32[256,512]{1,0:T(8,128)S(1)} %fusion.37), channel_id=1, source_target_pairs={{0,120},{8,0},{16,8},{24,16},{32,24},{40,32},{48,40},{56,48},{64,5... | collective-permute-start | bytes 1572872 | tf_op jit(solution)/shard_map/ppermute | solution.py:10
  174.4 12.5 %collective-permute-start.6 = (f32[256,512]{1,0:T(8,128)S(1)}, f32[256,512]{1,0:T(8,128)S(1)}, u32[]{:S(2)}, u32[]{:S(2)}) collective-permute-start(f32[256,512]{1,0:T(8,128)S(1)} %fusion.36), channel_id=1, source_target_pairs={{0,120},{8,0},{16,8},{24,16},{32,24},{40,32},{48,40},{56,48},{64,5... | collective-permute-start | bytes 1572872 | tf_op jit(solution)/shard_map/ppermute | solution.py:10
  187.6 92.5 %copy-start.3 = (f32[256,256]{1,0:T(8,128)}, f32[256,256]{1,0:T(8,128)S(1)}, u32[]{:S(2)}) copy-start(f32[256,256]{1,0:T(8,128)S(1)} %fusion.34) | copy-start | bytes 786436
  189.1 12.4 %collective-permute-start.7 = (f32[256,512]{1,0:T(8,128)S(1)}, f32[256,512]{1,0:T(8,128)S(1)}, u32[]{:S(2)}, u32[]{:S(2)}) collective-permute-start(f32[256,512]{1,0:T(8,128)S(1)} %get-tuple-element.6), channel_id=1, source_target_pairs={{0,8},{8,16},{16,24},{24,32},{32,40},{40,48},{48,56},{56,64},{64,7... | collective-permute-start | bytes 1572872 | tf_op jit(solution)/shard_map/ppermute | solution.py:10
  201.5 12.2 %collective-permute-start.8 = (f32[256,512]{1,0:T(8,128)S(1)}, f32[256,512]{1,0:T(8,128)S(1)}, u32[]{:S(2)}, u32[]{:S(2)}) collective-permute-start(f32[256,512]{1,0:T(8,128)S(1)} %collective-permute-done.7), channel_id=1, source_target_pairs={{0,8},{8,16},{16,24},{24,32},{32,40},{40,48},{48,56},{56,64},{64,7... | collective-permute-start | bytes 1572872 | tf_op jit(solution)/shard_map/ppermute | solution.py:10
  213.7 12.2 %collective-permute-start.9 = (f32[256,512]{1,0:T(8,128)S(1)}, f32[256,512]{1,0:T(8,128)S(1)}, u32[]{:S(2)}, u32[]{:S(2)}) collective-permute-start(f32[256,512]{1,0:T(8,128)S(1)} %collective-permute-done.8), channel_id=1, source_target_pairs={{0,8},{8,16},{16,24},{24,32},{32,40},{40,48},{48,56},{56,64},{64,7... | collective-permute-start | bytes 1572872 | tf_op jit(solution)/shard_map/ppermute | solution.py:10
  225.9 12.2 %collective-permute-start.10 = (f32[256,512]{1,0:T(8,128)S(1)}, f32[256,512]{1,0:T(8,128)S(1)}, u32[]{:S(2)}, u32[]{:S(2)}) collective-permute-start(f32[256,512]{1,0:T(8,128)S(1)} %collective-permute-done.9), channel_id=1, source_target_pairs={{0,8},{8,16},{16,24},{24,32},{32,40},{40,48},{48,56},{56,64},{64,7... | collective-permute-start | bytes 1572872 | tf_op jit(solution)/shard_map/ppermute | solution.py:10
  238.1 12.2 %collective-permute-start.11 = (f32[256,512]{1,0:T(8,128)S(1)}, f32[256,512]{1,0:T(8,128)S(1)}, u32[]{:S(2)}, u32[]{:S(2)}) collective-permute-start(f32[256,512]{1,0:T(8,128)S(1)} %collective-permute-done.10), channel_id=1, source_target_pairs={{0,8},{8,16},{16,24},{24,32},{32,40},{40,48},{48,56},{56,64},{64,7... | collective-permute-start | bytes 1572872 | tf_op jit(solution)/shard_map/ppermute | solution.py:10
  250.3 12.2 %collective-permute-start.12 = (f32[256,512]{1,0:T(8,128)S(1)}, f32[256,512]{1,0:T(8,128)S(1)}, u32[]{:S(2)}, u32[]{:S(2)}) collective-permute-start(f32[256,512]{1,0:T(8,128)S(1)} %collective-permute-done.11), channel_id=1, source_target_pairs={{0,8},{8,16},{16,24},{24,32},{32,40},{40,48},{48,56},{56,64},{64,7... | collective-permute-start | bytes 1572872 | tf_op jit(solution)/shard_map/ppermute | solution.py:10
  262.6 12.2 %collective-permute-start.13 = (f32[256,512]{1,0:T(8,128)S(1)}, f32[256,512]{1,0:T(8,128)S(1)}, u32[]{:S(2)}, u32[]{:S(2)}) collective-permute-start(f32[256,512]{1,0:T(8,128)S(1)} %collective-permute-done.12), channel_id=1, source_target_pairs={{0,8},{8,16},{16,24},{24,32},{32,40},{40,48},{48,56},{56,64},{64,7... | collective-permute-start | bytes 1572872 | tf_op jit(solution)/shard_map/ppermute | solution.py:10
  325.8 20.5 %copy-start.2 = (bf16[64,512,128]{2,1,0:T(8,128)(2,1)}, bf16[64,512,128]{2,1,0:T(8,128)(2,1)S(1)}, u32[]{:S(2)}) copy-start(bf16[64,512,128]{2,1,0:T(8,128)(2,1)S(1)} %fusion.1) | copy-start | bytes 25165828
  325.8 15.7 %slice-start = ((s8[8388608]{0:T(1024)(128)(4,1)}), s8[4194304]{0:T(1024)(128)(4,1)S(1)}, s32[]{:S(2)}) async-start(s8[8388608]{0:T(1024)(128)(4,1)} %bitcast.175), calls=%async_computation | async-start | bytes 8388608
  333.2 8.3 %slice-start.1 = ((s8[8388608]{0:T(1024)(128)(4,1)}), s8[4194304]{0:T(1024)(128)(4,1)S(1)}, s32[]{:S(2)}) async-start(s8[8388608]{0:T(1024)(128)(4,1)} %bitcast.175), calls=%async_computation.1 | async-start | bytes 8388608
  452.5 17.8 %copy-start.1 = (f32[256,64,8]{0,2,1:T(8,128)S(1)}, f32[256,64,8]{0,2,1:T(8,128)}, u32[]{:S(2)}) copy-start(f32[256,64,8]{0,2,1:T(8,128)} %param.12) | copy-start | bytes 1572868
